TPU v7x, 256 devices: a whole 4x4x8 slice. The times are simulated.
256 devices in a mesh: seq: 16 (over y, x), head: 8 (over z), dp: 2 (over core).
Axes of the slice: x: 4, y: 4, z: 8, core: 2. Of those that a mesh axis runs over, the one named last changes fastest.
Arguments:
- hidden: bfloat16 [8192, 2560], P(('dp', 'seq', 'head')), parts along dimension 0, may hold values from -6 to 6
- x_input: bfloat16 [8192, 5120], P(('dp', 'seq', 'head')), parts along dimension 0, may hold values from -6 to 6
- grad_out: bfloat16 [8192, 5120], P(('dp', 'seq', 'head')), parts along dimension 0, may hold values from -6 to 6
- bc_weight: bfloat16 [2560, 256], replicated, may hold values from -0.01953125 to 0.01953125
- dt_weight: bfloat16 [2560, 80], replicated, may hold values from -0.125 to 0.125
- dt_bias: float32 [80], replicated, may hold values from -3 to -2
- a_log: float32 [80], replicated, may hold values from -10 to -1.6
- d_skip: float32 [80], replicated, may hold values from 0.5 to 1.5
Outputs:
- mixer_out: bfloat16 [8192, 5120], P(('dp', 'seq', 'head')), parts along dimension 0
- grad_x: bfloat16 [8192, 5120], P(('dp', 'seq', 'head')), parts along dimension 0
- grad_hidden: bfloat16 [8192, 2560], P(('dp', 'seq', 'head')), parts along dimension 0
- grad_bc_weight: float32 [5120, 256], P('dp'), parts along dimension 0
- grad_dt_weight: float32 [5120, 80], P('dp'), parts along dimension 0
- param_grads: float32 [6, 80], P('dp'), parts along dimension 0
There are 2 independent parts, one for each index of `dp`. A program takes and returns all parts, laid end to end along the dimension named above; an argument that names none is the same for every part. Nothing has to cross between parts.
All inputs are finite; a program needn't handle non-finite values.
Results may differ from a plain program's by a relative error of at most 0.02.
Values may be sent and summed in bfloat16 or wider, within the bound.
No kernel may reach another device: no remote copies, remote signals or barrier semaphores. Data moves between devices by JAX's collectives and lax.ppermute only.
A program may use at most 128 MiB of HBM per device.

v0:
```python
import jax
import jax.numpy as jnp
from jax import lax
from jax.sharding import PartitionSpec as P

Q = 256
precise = lax.Precision.HIGHEST


def prefix_2(value, axis, combine, identity):
    devices, place = (lax.axis_size(axis), lax.axis_index(axis))
    everything = jax.tree.map(
        lambda part, kind: lax.all_gather(part.astype(kind), axis),
        value,
        (jnp.bfloat16, jnp.bfloat16),
    )
    start = jax.tree.map(
        lambda part, zero: jnp.broadcast_to(jnp.asarray(zero, part.dtype), part.shape),
        value,
        identity,
    )

    def step(k, before):
        reached = k < place
        new = combine(
            before, jax.tree.map(lambda part, own: part[k].astype(own.dtype), everything, value)
        )
        return jax.tree.map(lambda a, b: jnp.where(reached, a, b), new, before)

    return lax.fori_loop(0, devices, step, start)


def prefix_3(part, axis, combine, identity):
    count = lax.axis_size(axis)
    place = lax.axis_index(axis)
    ahead = count - 1 - place
    gathered = jax.tree.map(lambda a: lax.all_gather(a, axis), part)
    state = jax.tree.map(lambda a, e: jnp.zeros_like(a) + jnp.asarray(e, a.dtype), part, identity)

    def one(step, state):
        source = count - 1 - step
        return combine(
            state, jax.tree.map(lambda a: lax.dynamic_index_in_dim(a, source, 0, False), gathered)
        )

    return lax.fori_loop(0, ahead, one, state)


def span_scan(x_heads, step_size, b_rows, c_rows, neg_rate, state_in):
    length = x_heads.shape[0]
    blocks = length // Q
    heads_here = x_heads.shape[1]
    head_width = x_heads.shape[2]
    states = b_rows.shape[1]
    causal = (jnp.arange(Q)[:, None] >= jnp.arange(Q)[None, :])[:, :, None]

    def span_advance(carry, block):
        x_block, step_block, b_block, c_block = block
        running = jnp.cumsum(step_block * neg_rate[None, :], axis=0)
        scores = jnp.dot(c_block, b_block.T, precision=precise)
        spread = running[:, None, :] - running[None, :, :]
        decay = jnp.where(causal, jnp.exp(jnp.where(causal, spread, 0.0)), 0.0)
        scaled_x = x_block * step_block[:, :, None]
        inner = jnp.einsum("qkh,khp->qhp", decay * scores[:, :, None], scaled_x, precision=precise)
        carried = (
            jnp.einsum("qn,hnp->qhp", c_block, carry, precision=precise)
            * jnp.exp(running)[:, :, None]
        )
        total = running[-1]
        weights_end = jnp.exp(total[None, :] - running)
        fresh = jnp.einsum(
            "kn,khp->hnp", b_block, scaled_x * weights_end[:, :, None], precision=precise
        )
        return (jnp.exp(total)[:, None, None] * carry + fresh, inner + carried)

    pieces = (
        x_heads.reshape(blocks, Q, heads_here, head_width),
        step_size.reshape(blocks, Q, heads_here),
        b_rows.reshape(blocks, Q, states),
        c_rows.reshape(blocks, Q, states),
    )
    state_out, outputs = lax.scan(jax.checkpoint(span_advance), state_in, pieces)
    return (outputs.reshape(length, heads_here, head_width), state_out)


def mixer_local(x_heads, raw_step, b_rows, c_rows, log_decay, skip_gain, step_bias, state_in):
    step_size = jax.nn.softplus(raw_step + step_bias[None, :])
    neg_rate = -jnp.exp(log_decay)
    mixed, state_out = span_scan(x_heads, step_size, b_rows, c_rows, neg_rate, state_in)
    return (mixed + skip_gain[None, :, None] * x_heads, state_out)


def device_totals(x_heads, step_size, b_rows, c_rows, grad_heads, neg_rate):
    length = x_heads.shape[0]
    heads_here = x_heads.shape[1]
    head_width = x_heads.shape[2]
    states = b_rows.shape[1]
    blocks = length // Q

    def device_advance(carry, block):
        prefix, state_sum, adjoint_sum = carry
        x_block, step_block, b_block, c_block, grad_block = block
        running = jnp.cumsum(step_block * neg_rate[None, :], axis=0)
        total = running[-1]
        weights_end = jnp.exp(total[None, :] - running)
        scaled_x = x_block * step_block[:, :, None]
        fresh = jnp.einsum(
            "kn,khp->hnp", b_block, scaled_x * weights_end[:, :, None], precision=precise
        )
        state_sum = jnp.exp(total)[:, None, None] * state_sum + fresh
        reach = jnp.exp(prefix[None, :] + running)
        adjoint_sum = adjoint_sum + jnp.einsum(
            "qn,qhp->hnp", c_block, grad_block * reach[:, :, None], precision=precise
        )
        return ((prefix + total, state_sum, adjoint_sum), None)

    pieces = (
        x_heads.reshape(blocks, Q, heads_here, head_width),
        step_size.reshape(blocks, Q, heads_here),
        b_rows.reshape(blocks, Q, states),
        c_rows.reshape(blocks, Q, states),
        grad_heads.reshape(blocks, Q, heads_here, head_width),
    )
    start = (
        jnp.zeros((heads_here,), jnp.float32),
        jnp.zeros((heads_here, states, head_width), jnp.float32),
        jnp.zeros((heads_here, states, head_width), jnp.float32),
    )
    (prefix, state_sum, adjoint_sum), unused = lax.scan(device_advance, start, pieces)
    return (jnp.exp(prefix), state_sum, adjoint_sum)


def combine_pairs(earlier, later):
    return (earlier[0] * later[0], later[0][:, None, None] * earlier[1] + later[1])


def per_device(hidden, x_input, grad_out, bc_weight, dt_weight, dt_bias, a_log, d_skip):
    groups = lax.axis_size("head")
    head_index = lax.axis_index("head")
    heads_all = dt_weight.shape[1]
    heads_local = heads_all // groups
    head_width = x_input.shape[1] // heads_all
    states = bc_weight.shape[1] // 2
    proj_bc = jnp.dot(hidden, bc_weight, preferred_element_type=jnp.float32).astype(jnp.bfloat16)
    proj_dt = jnp.dot(hidden, dt_weight, preferred_element_type=jnp.float32).astype(jnp.bfloat16)
    x_local, raw_local, grad_local = (
        lax.all_to_all(x_input, "head", split_axis=1, concat_axis=0, tiled=True),
        lax.all_to_all(proj_dt, "head", split_axis=1, concat_axis=0, tiled=True),
        lax.all_to_all(grad_out, "head", split_axis=1, concat_axis=0, tiled=True),
    )
    bc_local = lax.all_gather(proj_bc, "head", axis=0, tiled=True)
    length = x_local.shape[0]
    x_heads = x_local.astype(jnp.float32).reshape(length, heads_local, head_width)
    grad_heads = grad_local.astype(jnp.float32).reshape(length, heads_local, head_width)
    raw_step = raw_local.astype(jnp.float32)
    b_rows = bc_local[:, :states].astype(jnp.float32)
    c_rows = bc_local[:, states:].astype(jnp.float32)
    offset = head_index * heads_local
    bias_local = lax.dynamic_slice_in_dim(dt_bias, offset, heads_local)
    log_local = lax.dynamic_slice_in_dim(a_log, offset, heads_local)
    skip_local = lax.dynamic_slice_in_dim(d_skip, offset, heads_local)
    step_size = jax.nn.softplus(raw_step + bias_local[None, :])
    neg_rate = -jnp.exp(log_local)
    decay_all, state_sum, adjoint_sum = device_totals(
        x_heads, step_size, b_rows, c_rows, grad_heads, neg_rate
    )
    identity = (
        jnp.ones((heads_local,), jnp.float32),
        jnp.zeros((heads_local, states, head_width), jnp.float32),
    )
    state_in = prefix_2((decay_all, state_sum), "seq", combine_pairs, identity)[1]
    state_grad = prefix_3((decay_all, adjoint_sum), "seq", combine_pairs, identity)[1]

    def forward(x_arg, raw_arg, b_arg, c_arg, log_arg, skip_arg, bias_arg):
        return mixer_local(x_arg, raw_arg, b_arg, c_arg, log_arg, skip_arg, bias_arg, state_in)

    (mixed, state_end), pullback = jax.vjp(
        forward, x_heads, raw_step, b_rows, c_rows, log_local, skip_local, bias_local
    )
    grad_xs, grad_raw, grad_b, grad_c, grad_alog, grad_skip, grad_bias = pullback(
        (grad_heads, state_grad)
    )
    out_local = mixed.reshape(length, heads_local * head_width).astype(jnp.bfloat16)
    gradx_local = grad_xs.reshape(length, heads_local * head_width).astype(jnp.bfloat16)
    step_local = grad_raw.astype(jnp.bfloat16)
    mixer_out, grad_x, d_step = (
        lax.all_to_all(out_local, "head", split_axis=0, concat_axis=1, tiled=True),
        lax.all_to_all(gradx_local, "head", split_axis=0, concat_axis=1, tiled=True),
        lax.all_to_all(step_local, "head", split_axis=0, concat_axis=1, tiled=True),
    )
    d_bc = lax.psum_scatter(
        jnp.concatenate([grad_b, grad_c], axis=1).astype(jnp.bfloat16),
        "head",
        scatter_dimension=0,
        tiled=True,
    )
    grad_hidden = (
        jnp.dot(d_bc, bc_weight.T, preferred_element_type=jnp.float32)
        + jnp.dot(d_step, dt_weight.T, preferred_element_type=jnp.float32)
    ).astype(jnp.bfloat16)
    seq_total = length * lax.axis_size("seq")
    weight_bc = jnp.dot(hidden.T, d_bc, preferred_element_type=jnp.float32) / seq_total
    weight_dt = jnp.dot(hidden.T, d_step, preferred_element_type=jnp.float32) / seq_total
    stacked = jnp.stack([grad_bias, grad_alog, grad_skip]) / seq_total
    param_local = lax.dynamic_update_slice(
        jnp.zeros((3, heads_all), jnp.float32), stacked, (0, offset)
    )
    grad_bc_weight, grad_dt_weight, param_grads = lax.psum(
        (weight_bc, weight_dt, param_local), ("seq", "head")
    )
    return (mixer_out, grad_x, grad_hidden, grad_bc_weight, grad_dt_weight, param_grads)


def solution(mesh):
    in_specs = (
        P(("dp", "seq", "head"), None),
        P(("dp", "seq", "head"), None),
        P(("dp", "seq", "head"), None),
        P(),
        P(),
        P(),
        P(),
        P(),
    )
    out_specs = (
        P(("dp", "seq", "head"), None),
        P(("dp", "seq", "head"), None),
        P(("dp", "seq", "head"), None),
        P("dp", None),
        P("dp", None),
        P("dp", None),
    )
    return jax.shard_map(
        per_device, mesh=mesh, in_specs=in_specs, out_specs=out_specs, check_vma=False
    )
```

profile of v0, /device:TPU:0, one launch (start us, length us, event | category | flops | bytes accessed | tf_op | source)
XLA Modules:
  0.0 757.0 jit_solution(9546356608684292287)
XLA Ops:
  9.5 6.7 all-to-all-start.1
  19.9 4.0 all-to-all-done.1
  23.9 3.4 all-to-all-start
  27.4 27.6 %all_gather.23 = bf16[256,256]{1,0:T(8,128)(2,1)S(1)} all-gather(bf16[32,256]{1,0:T(8,128)(2,1)S(1)} %convolution_convert_fusion), channel_id=1, replica_groups=mesh['seq'=16,'head'=8,'dp'=2] {'head'}, dimensions={0}, use_global_device_ids=true | all-gather | bytes 147456 | tf_op jit(solution)/shard_map/all_gather | solution.py:151
  57.0 6.1 all-to-all-start.3
  77.8 3.5 multiply_reduce_fusion
  91.4 20.9 %all-gather.2 = bf16[16,1,10]{2,1,0:T(2,128)(2,1)S(1)} all-gather(bf16[1,1,10]{2,1,0:T(2,128)(2,1)S(1)} %bitcast.278), channel_id=1, replica_groups=mesh['seq'=16,'head'=8,'dp'=2] {'seq'}, dimensions={0}, use_global_device_ids=true | all-gather | bytes 340 | tf_op jit(solution)/shard_map/all_gather | solution.py:13
  112.3 21.2 %all-gather.3 = f32[16,1,10]{2,1,0:T(1,128)} all-gather(f32[1,1,10]{2,1,0:T(1,128)} %bitcast.276), channel_id=1, replica_groups=mesh['seq'=16,'head'=8,'dp'=2] {'seq'}, dimensions={0}, use_global_device_ids=true | all-gather | bytes 680 | tf_op jit(solution)/shard_map/all_gather | solution.py:37
  139.1 22.0 %while.21 = (s32[]{:T(128)}, f32[10,128,64]{2,1,0:T(8,128)S(1)}, s32[]{:T(128)}, bf16[16,10]{1,0:T(8,128)(2,1)S(1)}, bf16[16,10,128,64]{2,3,1,0:T(8,128)(2,1)}, /*index=5*/s32[]{:T(128)}, s32[]{:T(128)}) while((s32[]{:T(128)}, f32[10,128,64]{2,1,0:T(8,128)S(1)}, s32[]{:T(128)}, bf16[16,10]{1,0:T(8,128)(2,1)S(1)}, ...), condition=%wide.region_3.4_spmd.clone, body=%wide.region_2.3_spmd.clone.sunk | while | flops 409614 | bytes 1474765 | solution.py:30
  161.1 41.3 %all-gather.9.cloned.1.call-done = f32[160,128,64]{1,2,0:T(8,128)} async-done(((f32[10,128,64]{1,2,0:T(8,128)}), f32[160,128,64]{1,2,0:T(8,128)}) %all-gather.9.cloned.1.call-update) | async-done | bytes 5242896 | tf_op jit(solution)/shard_map/all_gather | solution.py:37
  202.5 57.5 %while.20 = (s32[]{:T(128)}, f32[10,128,64]{2,1,0:T(8,128)S(1)}, s32[]{:T(128)}, f32[16,10]{1,0:T(8,128)}, f32[16,10,128,64]{2,3,1,0:T(8,128)}, /*index=5*/s32[]{:T(128)}, s32[]{:T(128)}, s32[]{:T(128)}, s32[]{:T(128)}) while((s32[]{:T(128)}, f32[10,128,64]{2,1,0:T(8,128)S(1)}, s32[]{:T(128)}, f32[16,10]{1,0:T(8,128)}, ...), condition=%wide.region_5.6_spmd, body=%wide.region_4.5_spmd.sunk | while | flops 163846 | bytes 2294027 | solution.py:46
  268.0 3.0 copy.262
  278.4 5.8 fusion.19
  284.3 3.9 multiply_reduce_fusion.3
  302.8 7.0 all-to-all-start.5
  310.7 6.8 all-to-all-done.5
  318.8 28.1 %reduce-scatter.4.cloned.1.call-done = bf16[32,256]{1,0:T(8,128)(2,1)} async-done(((bf16[256,256]{1,0:T(8,128)(2,1)}), bf16[32,256]{1,0:T(8,128)(2,1)}) %reduce-scatter.4.cloned.1.call-update) | async-done | bytes 16400
  350.5 3.6 broadcast_multiply_fusion.1
  354.8 6.0 fusion.48
  370.9 4.4 all-to-all-start.2
  375.6 14.4 %all-to-all-done.2 = bf16[8,32,640]{2,1,0:T(8,128)(2,1)S(1)} async-done(((bf16[8,32,640]{2,1,0:T(8,128)(2,1)}), bf16[8,32,640]{2,1,0:T(8,128)(2,1)S(1)}, u32[]{:S(2)}, u32[]{:S(2)}) %all-to-all-start.2) | async-done | bytes 327712 | tf_op jit(solution)/shard_map/all_to_all | solution.py:187
  390.0 3.4 all-to-all-start.4
  393.6 349.3 %psum.23 = f32[3,80]{1,0:T(4,128)} all-reduce(f32[3,80]{1,0:T(4,128)S(1)} %dynamic_update_slice.19), channel_id=1, replica_groups=mesh['seq'=16,'head'=8,'dp'=2] {'seq','head'}, use_global_device_ids=true, to_apply=%region_25.26 | all-reduce | flops 240 | bytes 1920 | tf_op jit(solution)/shard_map/psum | solution.py:208
  745.9 3.3 copy.269
  (357 shorter events, 166.7 us)
Async XLA Ops:
  7.2 9.0 %copy-start = (bf16[2560,256]{1,0:T(8,128)(2,1)S(1)}, bf16[2560,256]{1,0:T(8,128)(2,1)}, u32[]{:S(2)}) copy-start(bf16[2560,256]{1,0:T(8,128)(2,1)} %param.15) | copy-start | bytes 3932164
  7.2 47.8 %copy-start.45 = (f32[80]{0:T(128)S(1)}, f32[80]{0:T(128)}, u32[]{:S(2)}) copy-start(f32[80]{0:T(128)} %param.17) | copy-start | bytes 964
  7.2 47.9 %copy-start.14 = (bf16[32,5120]{1,0:T(8,128)(2,1)S(1)}, bf16[32,5120]{1,0:T(8,128)(2,1)}, u32[]{:S(2)}) copy-start(bf16[32,5120]{1,0:T(8,128)(2,1)} %param.14) | copy-start | bytes 983044
  9.5 14.5 %all-to-all-start.1 = ((bf16[8,2,160]{2,1,0:T(2,128)(2,1)}), bf16[8,2,160]{2,1,0:T(2,128)(2,1)S(1)}, u32[]{:S(2)}, u32[]{:S(2)}) async-start(bf16[8,2,160]{2,1,0:T(2,128)(2,1)} %reshape.399), calls=%async_computation.1 | async-start | bytes 16384 | tf_op jit(solution)/shard_map/all_to_all | solution.py:148
  18.2 46.4 %copy-start.34 = (f32[10]{0:T(128)}, f32[10]{0:T(128)S(1)}, u32[]{:S(2)}) copy-start(f32[10]{0:T(128)S(1)} %fusion.113) | copy-start | bytes 124
  23.9 33.0 %all-to-all-start = ((bf16[32,8,640]{2,0,1:T(8,128)(2,1)}), bf16[32,8,640]{2,0,1:T(8,128)(2,1)S(1)}, u32[]{:S(2)}, u32[]{:S(2)}) async-start(bf16[32,8,640]{2,0,1:T(8,128)(2,1)} %bitcast.236), calls=%async_computation | async-start | bytes 655360 | tf_op jit(solution)/shard_map/all_to_all | solution.py:147
  55.1 9.6 %copy-start.36 = (f32[10]{0:T(128)}, f32[10]{0:T(128)S(1)}, u32[]{:S(2)}) copy-start(f32[10]{0:T(128)S(1)} %dynamic_slice.73) | copy-start | bytes 124
  57.0 20.9 %all-to-all-start.3 = ((bf16[32,8,640]{2,0,1:T(8,128)(2,1)}), bf16[32,8,640]{2,0,1:T(8,128)(2,1)}, u32[]{:S(2)}, u32[]{:S(2)}) async-start(bf16[32,8,640]{2,0,1:T(8,128)(2,1)} %bitcast.235), calls=%async_computation.3 | async-start | bytes 655360 | tf_op jit(solution)/shard_map/all_to_all | solution.py:149
  63.0 76.1 %all-gather.7.cloned.1.call-start = ((), (), s32[]{:S(2)}) async-start(), calls=%async_computation.7 | async-start | bytes 2785280 | tf_op jit(solution)/shard_map/all_gather | solution.py:13
  85.5 117.0 %all-gather.9.cloned.1.call-start = ((), (), s32[]{:S(2)}) async-start(), calls=%async_computation.8 | async-start | bytes 5570560 | tf_op jit(solution)/shard_map/all_gather | solution.py:37
  90.5 176.4 %copy-start.3 = (f32[256,128]{1,0:T(8,128)}, f32[256,128]{1,0:T(8,128)S(1)}, u32[]{:S(2)}) copy-start(f32[256,128]{1,0:T(8,128)S(1)} %get-tuple-element.368) | copy-start | bytes 393220
  261.7 9.3 %copy-start.38 = (f32[10]{0:T(128)}, f32[10]{0:T(128)S(1)}, u32[]{:S(2)}) copy-start(f32[10]{0:T(128)S(1)} %slice_bitcast_fusion) | copy-start | bytes 124
  298.5 19.2 %copy-start.2 = (bf16[32,2560]{1,0:T(8,128)(2,1)S(1)}, bf16[32,2560]{1,0:T(8,128)(2,1)}, u32[]{:S(2)}) copy-start(bf16[32,2560]{1,0:T(8,128)(2,1)} %param.12) | copy-start | bytes 491524
  302.8 14.7 %all-to-all-start.5 = ((bf16[8,2,160]{2,1,0:T(2,128)(2,1)}), bf16[8,2,160]{2,1,0:T(2,128)(2,1)S(1)}, u32[]{:S(2)}, u32[]{:S(2)}) async-start(bf16[8,2,160]{2,1,0:T(2,128)(2,1)} %reshape.401), calls=%async_computation.5 | async-start | bytes 16384 | tf_op jit(solution)/shard_map/all_to_all | solution.py:189
  309.8 37.1 %reduce-scatter.4.cloned.1.call-start = ((), (), s32[]{:S(2)}) async-start(), calls=%async_computation.9 | async-start | bytes 147456
  310.7 435.2 %all-reduce.4.cloned.1.call-start = ((), (), s32[]{:S(2)}) async-start(), calls=%async_computation.10 | async-start | bytes 6881280 | tf_op jit(solution)/shard_map/psum | solution.py:208
  317.7 32.0 %copy-start.18 = (bf16[32,80]{0,1:T(8,128)(2,1)}, bf16[32,80]{0,1:T(8,128)(2,1)S(1)}, u32[]{:S(2)}) copy-start(bf16[32,80]{0,1:T(8,128)(2,1)S(1)} %all_to_all.80) | copy-start | bytes 15364
  318.8 30.8 %copy-start.46 = (f32[80]{0:T(128)S(1)}, f32[80]{0:T(128)}, u32[]{:S(2)}) copy-start(f32[80]{0:T(128)} %param.19) | copy-start | bytes 964
  368.3 25.2 %copy-start.40 = (f32[10]{0:T(128)S(1)}, f32[10]{0:T(128)}, u32[]{:S(2)}) copy-start(f32[10]{0:T(128)} %get-tuple-element.530) | copy-start | bytes 124
  368.3 374.6 %copy-start.24 = (bf16[32,256]{1,0:T(8,128)(2,1)S(1)}, bf16[32,256]{1,0:T(8,128)(2,1)}, u32[]{:S(2)}) copy-start(bf16[32,256]{1,0:T(8,128)(2,1)} %reduce-scatter.4.cloned.1.call-done) | copy-start | bytes 49156
  368.3 375.1 %copy-start.7 = (bf16[2560,80]{0,1:T(8,128)(2,1)S(1)}, bf16[2560,80]{0,1:T(8,128)(2,1)}, u32[]{:S(2)}) copy-start(bf16[2560,80]{0,1:T(8,128)(2,1)} %param.16) | copy-start | bytes 1228804
  368.3 375.1 %copy-start.19 = (bf16[32,80]{0,1:T(8,128)(2,1)S(1)}, bf16[32,80]{0,1:T(8,128)(2,1)}, u32[]{:S(2)}) copy-start(bf16[32,80]{0,1:T(8,128)(2,1)} %copy-done.18) | copy-start | bytes 15364
  370.9 19.1 %all-to-all-start.2 = ((bf16[8,32,640]{2,1,0:T(8,128)(2,1)}), bf16[8,32,640]{2,1,0:T(8,128)(2,1)S(1)}, u32[]{:S(2)}, u32[]{:S(2)}) async-start(bf16[8,32,640]{2,1,0:T(8,128)(2,1)} %get-tuple-element.546), calls=%async_computation.2 | async-start | bytes 655360 | tf_op jit(solution)/shard_map/all_to_all | solution.py:187
  390.0 355.1 %all-to-all-start.4 = ((bf16[8,32,640]{2,1,0:T(8,128)(2,1)}), bf16[8,32,640]{2,1,0:T(8,128)(2,1)S(1)}, u32[]{:S(2)}, u32[]{:S(2)}) async-start(bf16[8,32,640]{2,1,0:T(8,128)(2,1)} %get-tuple-element.545), calls=%async_computation.4 | async-start | bytes 655360 | tf_op jit(solution)/shard_map/all_to_all | solution.py:188
  (33 other events, 154.3 us)
Sparse Core Ops, SparseCore 0:
  85.6 52.9 all-gather.6
  141.6 60.7 all-gather.8
  313.7 33.1 reduce-scatter.3
  353.9 237.4 all-reduce.3
where the time goes:
time: 768 us; the launch traced here: 757 us
  blocking collectives  419 us (55%)
  local copies, waits for them, and re-layouts  124 us (16%)
  waiting for transfers between devices  94.7 us (12%)
  matrix products  38.5 us (5%)
  other arithmetic  32.8 us (4%)
  starting transfers between devices  31.3 us (4%)
  between operations  14.9 us (2%)
    psum x1, blocking collectives, per_device(): lax.psum((weight_bc, weight_dt, param_local), ('seq', 'head'))  349 us
    dynamic_slice x30, local copies, waits for them, and re-layouts, one(): lax.dynamic_index_in_dim(a, source, 0, False)  44 us
    all_gather x1, waiting for transfers between devices, prefix_3(): gathered = jax.tree.map(lambda a: lax.all_gather(a, axis), part)  41.3 us
    unnamed x5, waiting for transfers between devices  28.1 us
    all_gather x1, blocking collectives, per_device(): bc_local = lax.all_gather(proj_bc, 'head', axis=0, tiled=True)  27.6 us
    all_gather x1, blocking collectives, prefix_3(): gathered = jax.tree.map(lambda a: lax.all_gather(a, axis), part)  21.2 us
    all_gather x1, blocking collectives, prefix_2(): lax.all_gather(part.astype(kind), axis)  20.9 us
    dynamic_slice x32, local copies, waits for them, and re-layouts, step(): part[k].astype(own.dtype)  18.6 us
  transfers between devices with their start and end apart: 10, of which 5 were waited for; matrix products, arithmetic and copies ran while one was open for 10% of the time, Pallas kernels for 0%

commit v1 on v0

--- a/solution.py
+++ b/solution.py
@@ -1,3 +1,4 @@
+import functools
 import jax
 import jax.numpy as jnp
 from jax import lax
@@ -5,6 +6,15 @@
 
 Q = 256
 precise = lax.Precision.HIGHEST
+
+
+def move_the_copies(field, link_axis, ax_name):
+    for num in (link_axis, ax_name):
+        field = lax.psum(field, num)
+    return field
+
+
+replace_figure = functools.partial(move_the_copies, link_axis="head", ax_name="seq")
 
 
 def prefix_2(value, axis, combine, identity):
@@ -205,8 +215,8 @@
     param_local = lax.dynamic_update_slice(
         jnp.zeros((3, heads_all), jnp.float32), stacked, (0, offset)
     )
-    grad_bc_weight, grad_dt_weight, param_grads = lax.psum(
-        (weight_bc, weight_dt, param_local), ("seq", "head")
+    grad_bc_weight, grad_dt_weight, param_grads = replace_figure(
+        (weight_bc, weight_dt, param_local)
     )
     return (mixer_out, grad_x, grad_hidden, grad_bc_weight, grad_dt_weight, param_grads)
 

time: 768 us -> 582 us (0.76)
  the two profiles are of different devices: /device:TPU:0 before, /device:TPU:1 now
where the time goes in v1:
time: 582 us; the launch traced here: 571 us
  waiting for transfers between devices  208 us (36%)
  local copies, waits for them, and re-layouts  130 us (22%)
  blocking collectives  105 us (18%)
  matrix products  39.7 us (7%)
  other arithmetic  38.8 us (7%)
  starting transfers between devices  32.9 us (6%)
  between operations  14.8 us (3%)
    psum x2, waiting for transfers between devices, move_the_copies(): field = lax.psum(field, num)  119 us
    psum x2, blocking collectives, move_the_copies(): field = lax.psum(field, num)  49.1 us
    dynamic_slice x30, local copies, waits for them, and re-layouts, one(): lax.dynamic_index_in_dim(a, source, 0, False)  44 us
    all_gather x1, waiting for transfers between devices, prefix_3(): gathered = jax.tree.map(lambda a: lax.all_gather(a, axis), part)  32.1 us
    unnamed x6, waiting for transfers between devices  24.1 us
    all_gather x1, blocking collectives, per_device(): bc_local = lax.all_gather(proj_bc, 'head', axis=0, tiled=True)  22.7 us
    dynamic_slice x32, local copies, waits for them, and re-layouts, step(): part[k].astype(own.dtype)  18.6 us
    all_gather x1, blocking collectives, prefix_3(): gathered = jax.tree.map(lambda a: lax.all_gather(a, axis), part)  16.7 us
  transfers between devices with their start and end apart: 11, of which 8 were waited for; matrix products, arithmetic and copies ran while one was open for 16% of the time, Pallas kernels for 0%

profile of v1, /device:TPU:1, one launch (start us, length us, event | category | flops | bytes accessed | tf_op | source)
XLA Modules:
  0.0 570.7 jit_solution(15210609173691321867)
XLA Ops:
  9.5 9.0 %all-to-all-start.1 = ((bf16[8,2,160]{2,1,0:T(2,128)(2,1)}), bf16[8,2,160]{2,1,0:T(2,128)(2,1)S(1)}, u32[]{:S(2)}, u32[]{:S(2)}) async-start(bf16[8,2,160]{2,1,0:T(2,128)(2,1)} %reshape.399), calls=%async_computation.1 | async-start | bytes 16384 | tf_op jit(solution)/shard_map/all_to_all | solution.py:158
  25.1 3.8 all-to-all-start
  28.9 22.7 %all_gather.23 = bf16[256,256]{1,0:T(8,128)(2,1)S(1)} all-gather(bf16[32,256]{1,0:T(8,128)(2,1)S(1)} %convolution_convert_fusion), channel_id=1, replica_groups=mesh['seq'=16,'head'=8,'dp'=2] {'head'}, dimensions={0}, use_global_device_ids=true | all-gather | bytes 147456 | tf_op jit(solution)/shard_map/all_gather | solution.py:161
  53.5 5.8 %all-to-all-start.3 = ((bf16[32,8,640]{2,0,1:T(8,128)(2,1)}), bf16[32,8,640]{2,0,1:T(8,128)(2,1)S(1)}, u32[]{:S(2)}, u32[]{:S(2)}) async-start(bf16[32,8,640]{2,0,1:T(8,128)(2,1)} %bitcast.235), calls=%async_computation.3 | async-start | bytes 655360 | tf_op jit(solution)/shard_map/all_to_all | solution.py:159
  79.4 3.6 fusion.62
  84.8 3.6 fusion.56
  90.7 16.3 %all-gather.2 = bf16[16,1,10]{2,1,0:T(2,128)(2,1)S(1)} all-gather(bf16[1,1,10]{2,1,0:T(2,128)(2,1)S(1)} %bitcast.278), channel_id=1, replica_groups=mesh['seq'=16,'head'=8,'dp'=2] {'seq'}, dimensions={0}, use_global_device_ids=true | all-gather | bytes 340 | tf_op jit(solution)/shard_map/all_gather | solution.py:23
  107.6 16.7 %all-gather.3 = f32[16,1,10]{2,1,0:T(1,128)} all-gather(f32[1,1,10]{2,1,0:T(1,128)} %bitcast.276), channel_id=1, replica_groups=mesh['seq'=16,'head'=8,'dp'=2] {'seq'}, dimensions={0}, use_global_device_ids=true | all-gather | bytes 680 | tf_op jit(solution)/shard_map/all_gather | solution.py:47
  127.9 13.9 %all-gather.7.cloned.1.call-done = bf16[160,128,64]{1,2,0:T(8,128)(2,1)} async-done(((bf16[10,128,64]{1,2,0:T(8,128)(2,1)}), bf16[160,128,64]{1,2,0:T(8,128)(2,1)}) %all-gather.7.cloned.1.call-update) | async-done | bytes 2621456 | tf_op jit(solution)/shard_map/all_gather | solution.py:23
  141.9 32.3 %while.21 = (s32[]{:T(128)}, f32[10,128,64]{2,1,0:T(8,128)S(1)}, s32[]{:T(128)}, bf16[16,10]{1,0:T(8,128)(2,1)}, bf16[16,10,128,64]{2,3,1,0:T(8,128)(2,1)}, /*index=5*/s32[]{:T(128)}, s32[]{:T(128)}) while((s32[]{:T(128)}, f32[10,128,64]{2,1,0:T(8,128)S(1)}, s32[]{:T(128)}, bf16[16,10]{1,0:T(8,128)(2,1)}, ...), condition=%wide.region_3.4_spmd.clone, body=%wide.region_2.3_spmd.clone.sunk | while | flops 409614 | bytes 1474765 | solution.py:40
  174.2 32.1 %all-gather.9.cloned.1.call-done = f32[160,128,64]{1,2,0:T(8,128)} async-done(((f32[10,128,64]{1,2,0:T(8,128)}), f32[160,128,64]{1,2,0:T(8,128)}) %all-gather.9.cloned.1.call-update) | async-done | bytes 5242896 | tf_op jit(solution)/shard_map/all_gather | solution.py:47
  206.3 57.9 %while.20 = (s32[]{:T(128)}, f32[10,128,64]{2,1,0:T(8,128)S(1)}, s32[]{:T(128)}, f32[16,10]{1,0:T(8,128)}, f32[16,10,128,64]{2,3,1,0:T(8,128)}, /*index=5*/s32[]{:T(128)}, s32[]{:T(128)}, s32[]{:T(128)}, s32[]{:T(128)}) while((s32[]{:T(128)}, f32[10,128,64]{2,1,0:T(8,128)S(1)}, s32[]{:T(128)}, f32[16,10]{1,0:T(8,128)}, ...), condition=%wide.region_5.6_spmd, body=%wide.region_4.5_spmd.sunk | while | flops 163846 | bytes 2294027 | solution.py:56
  283.5 6.0 %fusion.19 = (f32[256,10]{0,1:T(8,128)S(1)}, f32[256,10]{0,1:T(8,128)}, f32[256,256]{1,0:T(8,128)}) fusion(f32[256,256]{1,0:T(8,128)} %fusion.116, f32[256,10]{0,1:T(8,128)S(1)} %copy.249, pred[256,256]{1,0:T(8,128)(4,1)} %bitcast.268, f32[10,64,256]{2,1,0:T(8,128)} %copy.251, f32[256,10,64]{0,2,1:T(8,128)} %copy.254, f32[256,10]{0,1:T(8,128)S(1)} %get-tuple-element.364), kind=kOutput, calls=%fused_computation.30 | convolution fusion | flops 510618624 | bytes 1941504 | tf_op jit(solution)/shard_map/transpose(jvp())/while/body/eval_jaxpr/checkpoint/qkh,khp->qhp/dot_general | solution.py:74
  289.5 3.9 multiply_reduce_fusion.3
  308.2 6.7 %all-to-all-start.5 = ((bf16[8,2,160]{2,1,0:T(2,128)(2,1)}), bf16[8,2,160]{2,1,0:T(2,128)(2,1)S(1)}, u32[]{:S(2)}, u32[]{:S(2)}) async-start(bf16[8,2,160]{2,1,0:T(2,128)(2,1)} %reshape.401), calls=%async_computation.5 | async-start | bytes 16384 | tf_op jit(solution)/shard_map/all_to_all | solution.py:199
  315.8 5.7 all-to-all-done.5
  322.8 24.0 %reduce-scatter.4.cloned.1.call-done = bf16[32,256]{1,0:T(8,128)(2,1)} async-done(((bf16[256,256]{1,0:T(8,128)(2,1)}), bf16[32,256]{1,0:T(8,128)(2,1)}) %reduce-scatter.4.cloned.1.call-update) | async-done | bytes 16400
  349.6 100.4 %all-reduce.8.cloned.1.call-done = (f32[2560,256]{0,1:T(8,128)}, f32[2560,80]{0,1:T(8,128)}) async-done(((f32[2560,256]{0,1:T(8,128)}, f32[2560,80]{0,1:T(8,128)}), (f32[2560,256]{0,1:T(8,128)}, f32[2560,80]{0,1:T(8,128)})) %all-reduce.8.cloned.1.call-update) | async-done | bytes 3440656 | tf_op jit(solution)/shard_map/psum | solution.py:13
  454.8 5.2 fusion.48
  470.5 4.0 all-to-all-start.2
  474.8 11.2 %all-to-all-done.2 = bf16[8,32,640]{2,1,0:T(8,128)(2,1)S(1)} async-done(((bf16[8,32,640]{2,1,0:T(8,128)(2,1)}), bf16[8,32,640]{2,1,0:T(8,128)(2,1)S(1)}, u32[]{:S(2)}, u32[]{:S(2)}) %all-to-all-start.2) | async-done | bytes 327712 | tf_op jit(solution)/shard_map/all_to_all | solution.py:197
  489.5 15.1 %psum.46 = f32[3,80]{1,0:T(4,128)S(1)} all-reduce(f32[3,80]{1,0:T(4,128)S(1)} %dynamic_update_slice.19), channel_id=1, replica_groups=mesh['seq'=16,'head'=8,'dp'=2] {'head'}, use_global_device_ids=true, to_apply=%region_27.28 | all-reduce | flops 240 | bytes 1920 | tf_op jit(solution)/shard_map/psum | solution.py:13
  504.7 34.0 %psum.47 = f32[3,80]{1,0:T(4,128)} all-reduce(f32[3,80]{1,0:T(4,128)S(1)} %psum.46), channel_id=1, replica_groups=mesh['seq'=16,'head'=8,'dp'=2] {'seq'}, use_global_device_ids=true, to_apply=%region_28.29 | all-reduce | flops 240 | bytes 1920 | tf_op jit(solution)/shard_map/psum | solution.py:13
  541.6 18.2 %all-reduce.6.cloned.1.call-done = (f32[2560,256]{0,1:T(8,128)}, f32[2560,80]{0,1:T(8,128)}) async-done(((f32[2560,256]{0,1:T(8,128)}, f32[2560,80]{0,1:T(8,128)}), (f32[2560,256]{0,1:T(8,128)}, f32[2560,80]{0,1:T(8,128)})) %all-reduce.6.cloned.1.call-update) | async-done | bytes 3440656 | tf_op jit(solution)/shard_map/psum | solution.py:13
  (347 shorter events, 192.6 us)
Async XLA Ops:
  7.2 11.3 %copy-start = (bf16[2560,256]{1,0:T(8,128)(2,1)S(1)}, bf16[2560,256]{1,0:T(8,128)(2,1)}, u32[]{:S(2)}) copy-start(bf16[2560,256]{1,0:T(8,128)(2,1)} %param.15) | copy-start | bytes 3932164
  7.2 44.3 %copy-start.38 = (f32[80]{0:T(128)S(1)}, f32[80]{0:T(128)}, u32[]{:S(2)}) copy-start(f32[80]{0:T(128)} %param.17) | copy-start | bytes 964
  7.2 44.4 %copy-start.18 = (bf16[32,5120]{1,0:T(8,128)(2,1)S(1)}, bf16[32,5120]{1,0:T(8,128)(2,1)}, u32[]{:S(2)}) copy-start(bf16[32,5120]{1,0:T(8,128)(2,1)} %param.14) | copy-start | bytes 983044
  9.5 15.6 %all-to-all-start.1 = ((bf16[8,2,160]{2,1,0:T(2,128)(2,1)}), bf16[8,2,160]{2,1,0:T(2,128)(2,1)S(1)}, u32[]{:S(2)}, u32[]{:S(2)}) async-start(bf16[8,2,160]{2,1,0:T(2,128)(2,1)} %reshape.399), calls=%async_computation.1 | async-start | bytes 16384 | tf_op jit(solution)/shard_map/all_to_all | solution.py:158
  20.5 32.2 %copy-start.32 = (f32[10]{0:T(128)}, f32[10]{0:T(128)S(1)}, u32[]{:S(2)}) copy-start(f32[10]{0:T(128)S(1)} %fusion.113) | copy-start | bytes 124
  25.1 28.4 %all-to-all-start = ((bf16[32,8,640]{2,0,1:T(8,128)(2,1)}), bf16[32,8,640]{2,0,1:T(8,128)(2,1)S(1)}, u32[]{:S(2)}, u32[]{:S(2)}) async-start(bf16[32,8,640]{2,0,1:T(8,128)(2,1)} %bitcast.236), calls=%async_computation | async-start | bytes 655360 | tf_op jit(solution)/shard_map/all_to_all | solution.py:157
  51.6 8.8 %copy-start.34 = (f32[10]{0:T(128)}, f32[10]{0:T(128)S(1)}, u32[]{:S(2)}) copy-start(f32[10]{0:T(128)S(1)} %dynamic_slice.73) | copy-start | bytes 124
  53.5 70.7 %copy-start.1 = (bf16[32,8,640]{2,0,1:T(8,128)(2,1)}, bf16[32,8,640]{2,0,1:T(8,128)(2,1)S(1)}, u32[]{:S(2)}) copy-start(bf16[32,8,640]{2,0,1:T(8,128)(2,1)S(1)} %all-to-all-done) | copy-start | bytes 983044
  53.5 20.2 %all-to-all-start.3 = ((bf16[32,8,640]{2,0,1:T(8,128)(2,1)}), bf16[32,8,640]{2,0,1:T(8,128)(2,1)S(1)}, u32[]{:S(2)}, u32[]{:S(2)}) async-start(bf16[32,8,640]{2,0,1:T(8,128)(2,1)} %bitcast.235), calls=%async_computation.3 | async-start | bytes 655360 | tf_op jit(solution)/shard_map/all_to_all | solution.py:159
  59.3 82.6 %all-gather.7.cloned.1.call-start = ((), (), s32[]{:S(2)}) async-start(), calls=%async_computation.7 | async-start | bytes 2785280 | tf_op jit(solution)/shard_map/all_gather | solution.py:23
  73.7 52.4 %copy-start.3 = (bf16[32,8,640]{2,0,1:T(8,128)(2,1)}, bf16[32,8,640]{2,0,1:T(8,128)(2,1)S(1)}, u32[]{:S(2)}) copy-start(bf16[32,8,640]{2,0,1:T(8,128)(2,1)S(1)} %all-to-all-done.3) | copy-start | bytes 983044
  83.0 123.3 %all-gather.9.cloned.1.call-start = ((), (), s32[]{:S(2)}) async-start(), calls=%async_computation.8 | async-start | bytes 5570560 | tf_op jit(solution)/shard_map/all_gather | solution.py:47
  266.0 8.9 %copy-start.36 = (f32[10]{0:T(128)}, f32[10]{0:T(128)S(1)}, u32[]{:S(2)}) copy-start(f32[10]{0:T(128)S(1)} %slice_bitcast_fusion) | copy-start | bytes 124
  304.5 17.2 %copy-start.7 = (bf16[32,2560]{1,0:T(8,128)(2,1)S(1)}, bf16[32,2560]{1,0:T(8,128)(2,1)}, u32[]{:S(2)}) copy-start(bf16[32,2560]{1,0:T(8,128)(2,1)} %param.12) | copy-start | bytes 491524
  308.2 13.3 %all-to-all-start.5 = ((bf16[8,2,160]{2,1,0:T(2,128)(2,1)}), bf16[8,2,160]{2,1,0:T(2,128)(2,1)S(1)}, u32[]{:S(2)}, u32[]{:S(2)}) async-start(bf16[8,2,160]{2,1,0:T(2,128)(2,1)} %reshape.401), calls=%async_computation.5 | async-start | bytes 16384 | tf_op jit(solution)/shard_map/all_to_all | solution.py:199
  314.9 31.9 %reduce-scatter.4.cloned.1.call-start = ((), (), s32[]{:S(2)}) async-start(), calls=%async_computation.9 | async-start | bytes 147456
  315.8 134.3 %all-reduce.8.cloned.1.call-start = ((), (), s32[]{:S(2)}) async-start(), calls=%async_computation.11 | async-start | bytes 6881280 | tf_op jit(solution)/shard_map/psum | solution.py:13
  349.5 100.5 %copy-start.39 = (f32[80]{0:T(128)S(1)}, f32[80]{0:T(128)}, u32[]{:S(2)}) copy-start(f32[80]{0:T(128)} %param.19) | copy-start | bytes 964
  349.6 101.0 %copy-start.11 = (f32[256,10]{1,0:T(8,128)S(1)}, f32[256,10]{1,0:T(8,128)}, u32[]{:S(2)}) copy-start(f32[256,10]{1,0:T(8,128)} %copy-done.10) | copy-start | bytes 30724
  349.6 210.2 %all-reduce.6.cloned.1.call-start = ((), (), s32[]{:S(2)}) async-start(), calls=%async_computation.10 | async-start | bytes 6881280 | tf_op jit(solution)/shard_map/psum | solution.py:13
  469.5 69.2 %copy-start.26 = (bf16[32,256]{1,0:T(8,128)(2,1)S(1)}, bf16[32,256]{1,0:T(8,128)(2,1)}, u32[]{:S(2)}) copy-start(bf16[32,256]{1,0:T(8,128)(2,1)} %reduce-scatter.4.cloned.1.call-done) | copy-start | bytes 49156
  470.5 68.7 %copy-start.9 = (bf16[2560,80]{0,1:T(8,128)(2,1)S(1)}, bf16[2560,80]{0,1:T(8,128)(2,1)}, u32[]{:S(2)}) copy-start(bf16[2560,80]{0,1:T(8,128)(2,1)} %param.16) | copy-start | bytes 1228804
  470.5 15.4 %all-to-all-start.2 = ((bf16[8,32,640]{2,1,0:T(8,128)(2,1)}), bf16[8,32,640]{2,1,0:T(8,128)(2,1)S(1)}, u32[]{:S(2)}, u32[]{:S(2)}) async-start(bf16[8,32,640]{2,1,0:T(8,128)(2,1)} %get-tuple-element.548), calls=%async_computation.2 | async-start | bytes 655360 | tf_op jit(solution)/shard_map/all_to_all | solution.py:197
  485.9 54.9 %all-to-all-start.4 = ((bf16[8,32,640]{2,1,0:T(8,128)(2,1)}), bf16[8,32,640]{2,1,0:T(8,128)(2,1)S(1)}, u32[]{:S(2)}, u32[]{:S(2)}) async-start(bf16[8,32,640]{2,1,0:T(8,128)(2,1)} %get-tuple-element.547), calls=%async_computation.4 | async-start | bytes 655360 | tf_op jit(solution)/shard_map/all_to_all | solution.py:198
  (27 other events, 132.0 us)
Sparse Core Ops, SparseCore 0:
  83.1 58.7 all-gather.6
  144.9 61.3 all-gather.8
  318.8 27.9 reduce-scatter.3
  349.9 100.1 all-reduce.7
  453.4 106.2 all-reduce.5
